TPU v7x, 32 devices: a whole 2x2x4 slice. The times are simulated.
32 devices in a mesh: pods: 2 (over y), inst: 4 (over z), tp: 4 (over x, core).
Axes of the slice: x: 2, y: 2, z: 4, core: 2. Of those that a mesh axis runs over, the one named last changes fastest.
Arguments:
- queries: bfloat16 [2048, 4096], P(('pods', 'inst'), 'tp'), parts along dimension 0, may hold values from -62 to 62
- cache_store: bfloat16 [2, 2048, 16, 512], P(None, ('pods', 'inst'), None, 'tp'), parts along dimension 1, may hold values from -6 to 6
- span_cache: bfloat16 [2, 2048, 512], P(None, ('pods', 'inst'), 'tp'), parts along dimension 1, may hold values from -6 to 6
- out_weight: bfloat16 [4096, 4096], P('tp'), may hold values from -0.5 to 0.5
- prefix_blocks: int32 [8], P(('pods', 'inst')), parts along dimension 0, may hold values from 1 to 512, 1280 in all
- span_lengths: int32 [8], P(('pods', 'inst')), parts along dimension 0, may hold values from 1 to 256, 768 in all
- hit_holders: int32 [8, 512, 1], P(('pods', 'inst')), parts along dimension 0, may hold values from 0 to 3; in each aligned block of 512 rows (0 to 511, 512 to 1023, ..., all dimensions but the last counted through in order) at most 160 rows name the same one
- hit_slots: int32 [8, 512], P(('pods', 'inst')), parts along dimension 0, may hold values from 0 to 255
- store_owners: int32 [8, 16, 1], P(('pods', 'inst')), parts along dimension 0, may hold values from 0 to 3; in each aligned block of 16 rows (0 to 15, 16 to 31, ..., all dimensions but the last counted through in order) at most 8 rows name the same one
Outputs:
- projected: bfloat16 [2048, 4096], P(('pods', 'inst', 'tp')), parts along dimension 0
- pushed_blocks: bfloat16 [2, 256, 16, 512], P(None, ('pods', 'inst'), None, 'tp'), parts along dimension 1
There are 2 independent parts, one for each index of `pods`. A program takes and returns all parts, laid end to end along the dimension named above; an argument that names none is the same for every part. Nothing has to cross between parts.
Inputs may be any that keep to these rules, and one draw needn't show every extreme that they name: `prefix_blocks`: the largest equals 512; they sum to 1280. `span_lengths`: the largest equals 256; they sum to 768. `hit_holders`: among the 512 entries of one instance no holder appears more than 160 times, and some instance names some holder exactly 160 times. Entries past the live prefix are present too. `store_owners`: among the 16 blocks of one instance no owner appears more than 8 times, and some instance names some owner exactly 8 times.
All inputs are finite; a program needn't handle non-finite values. No bound on the sum of `prefix_blocks` or of `span_lengths` on one device may be relied on, other than what follows from the above.
Results may differ from a plain program's by a relative error of at most 0.013.
Values may be sent and summed in bfloat16 or wider, within the bound.
No kernel may reach another device: no remote copies, remote signals or barrier semaphores. Data moves between devices by JAX's collectives and lax.ppermute only.
A program may use at most 128 MiB of HBM per device.

v0:
```python
import math

import jax
import jax.numpy as jnp
from jax import lax
from jax.sharding import PartitionSpec as P


def slot_ranks(labels, number):
    onehot = (labels[:, None] == jnp.arange(number, dtype=jnp.int32)[None, :]).astype(jnp.int32)
    before = jnp.cumsum(onehot, axis=0) - onehot
    return jnp.sum(before * onehot, axis=1)


def absorb(carry_state, query_heads, key_rows, value_rows, usable):
    running_max, running_sum, running_out = carry_state
    scores = jnp.einsum(
        "thd,kd->htk", query_heads, key_rows, preferred_element_type=jnp.float32
    ) / math.sqrt(query_heads.shape[2])
    new_max = jnp.maximum(running_max, jnp.max(jnp.where(usable, scores, -1e30), axis=-1))
    weights = jnp.where(usable, jnp.exp(scores - new_max[..., None]), 0.0)
    rescale = jnp.exp(running_max - new_max)
    running_sum = running_sum * rescale + jnp.sum(weights, axis=-1)
    update = jnp.einsum(
        "htk,kd->htd", weights.astype(jnp.bfloat16), value_rows, preferred_element_type=jnp.float32
    )
    running_out = running_out * rescale[..., None] + update
    return (new_max, running_sum, running_out)


def shards(
    queries,
    cache_store,
    span_cache,
    out_weight,
    prefix_blocks,
    span_lengths,
    hit_holders,
    hit_slots,
    store_owners,
):
    peer_count = lax.axis_size("inst")
    block_rows = cache_store.shape[2]
    head_dim = cache_store.shape[3]
    span_rows = queries.shape[0]
    heads_here = queries.shape[1] // head_dim
    block_max = hit_slots.shape[1]
    pull_cap = max(2, block_max * 5 // (4 * peer_count))
    cap_pad = -(-pull_cap // pull_cap) * pull_cap
    entry_index = jnp.arange(block_max, dtype=jnp.int32)
    holders = hit_holders[0, :, 0]
    alive = jnp.ones((block_max,), bool)
    labels = jnp.where(alive, holders, peer_count)
    ranks = slot_ranks(labels, peer_count)
    place = jnp.where(alive, ranks, cap_pad)
    clamped = jnp.minimum(labels, peer_count - 1)
    prefix_live = entry_index < prefix_blocks[0]
    slot_live = (
        jnp.zeros((peer_count, cap_pad), bool).at[clamped, place].set(prefix_live, mode="drop")
    )
    wanted = (
        jnp.zeros((peer_count, cap_pad), jnp.int32)
        .at[clamped, place]
        .set(hit_slots[0], mode="drop")
    )
    wanted = lax.all_to_all(wanted, "inst", split_axis=0, concat_axis=0, tiled=True)
    picked = jnp.take(cache_store, wanted.reshape(-1), axis=1).reshape(
        2, peer_count, cap_pad, block_rows, head_dim
    )
    query_heads = queries.reshape(span_rows, heads_here, head_dim)
    span_live = span_lengths[0]
    init_state = (
        jnp.full((heads_here, span_rows), -1e30, jnp.float32),
        jnp.zeros((heads_here, span_rows), jnp.float32),
        jnp.zeros((heads_here, span_rows, head_dim), jnp.float32),
    )
    arrived = lax.all_to_all(picked, "inst", split_axis=1, concat_axis=1, tiled=True)

    def peer_step(peer_index, carry_state):
        rows_here = lax.dynamic_index_in_dim(arrived, peer_index, 1, keepdims=False).reshape(
            2, cap_pad * block_rows, head_dim
        )
        mask_row = lax.dynamic_index_in_dim(slot_live, peer_index, 0, keepdims=False)
        usable = jnp.broadcast_to(mask_row[:, None], (cap_pad, block_rows)).reshape(-1)
        return absorb(carry_state, query_heads, rows_here[0], rows_here[1], usable[None, None, :])

    carry_state = lax.fori_loop(0, peer_count, peer_step, init_state)
    column = jnp.arange(span_rows, dtype=jnp.int32)
    span_ok = (column[None, :] <= column[:, None]) & (column[None, :] < span_live)
    carry_state = absorb(
        carry_state, query_heads, span_cache[0], span_cache[1], span_ok[None, :, :]
    )
    final_max, final_sum, final_out = carry_state
    attended = (
        jnp.transpose(final_out / final_sum[..., None], (1, 0, 2))
        .reshape(span_rows, heads_here * head_dim)
        .astype(jnp.bfloat16)
    )
    own_rows = span_rows // lax.axis_size("tp")
    summed = lax.psum_scatter(
        jnp.dot(attended, out_weight, preferred_element_type=jnp.float32).astype(jnp.bfloat16),
        "tp",
        scatter_dimension=0,
        tiled=True,
    ).astype(jnp.float32)
    positions = lax.axis_index("tp") * own_rows + jnp.arange(own_rows, dtype=jnp.int32)
    projected = jnp.where((positions < span_live)[:, None], summed, 0.0).astype(jnp.bfloat16)
    new_count = span_rows // block_rows
    push_cap = max(2, 2 * new_count // peer_count)
    live_rows = column < span_live
    fresh_cache = jnp.where(
        live_rows[None, :, None], span_cache, jnp.zeros_like(span_cache)
    ).reshape(2, new_count, block_rows, head_dim)
    targets = store_owners[0, :, 0]
    push_ranks = slot_ranks(targets, peer_count)
    outgoing = (
        jnp.zeros((2, peer_count, push_cap, block_rows, head_dim), jnp.bfloat16)
        .at[:, targets, push_ranks]
        .set(fresh_cache)
    )
    incoming = lax.all_to_all(outgoing, "inst", split_axis=1, concat_axis=1, tiled=True)
    pushed_blocks = incoming.reshape(2, peer_count * push_cap, block_rows, head_dim)
    return (projected, pushed_blocks)


def solution(mesh):
    return jax.shard_map(
        shards,
        mesh=mesh,
        in_specs=(
            P(("pods", "inst"), "tp"),
            P(None, ("pods", "inst"), None, "tp"),
            P(None, ("pods", "inst"), "tp"),
            P("tp", None),
            P(("pods", "inst")),
            P(("pods", "inst")),
            P(("pods", "inst"), None, None),
            P(("pods", "inst"), None),
            P(("pods", "inst"), None, None),
        ),
        out_specs=(P(("pods", "inst", "tp"), None), P(None, ("pods", "inst"), None, "tp")),
        check_vma=False,
    )
```

profile of v0, /device:TPU:4, one launch (start us, length us, event | category | flops | bytes accessed | tf_op | source)
XLA Modules:
  0.0 365.5 jit_solution(9084822669289242675)
XLA Ops:
  7.2 0.8 fusion.36
  8.0 1.2 reduce-window.6
  9.7 0.7 fusion.34
  10.4 0.7 or_select_fusion
  11.1 42.5 %scatter_fusion.1 = s32[4,160]{1,0:T(4,128)S(1)} fusion(s32[4,160]{1,0:T(4,128)S(1)} %broadcast_in_dim.166, s32[512]{0:T(512)S(1)} %bitcast.131, s32[512]{0:T(512)} %bitcast.146), kind=kCustom, calls=%fused_computation.2 | custom fusion | bytes 10240 | tf_op jit(solution)/shard_map/scatter | solution.py:64
  53.7 10.2 %all_to_all.19 = s32[4,1,160]{2,1,0:T(1,128)S(1)} all-to-all(s32[4,1,160]{2,1,0:T(1,128)S(1)} %copy.49), channel_id=1, replica_groups=mesh['pods'=2,'inst'=4,'tp'=4] {'inst'}, dimensions={0} | all-to-all | bytes 5120 | tf_op jit(solution)/shard_map/all_to_all | solution.py:66
  64.1 4.1 %gather_fusion = bf16[640,2,16,128]{3,2,1,0:T(8,128)(2,1)} fusion(bf16[2,256,16,128]{3,2,1,0:T(8,128)(2,1)S(1)} %copy-done, s32[1024]{0:T(1024)S(1)} %pad_clamp_fusion), kind=kCustom, calls=%fused_computation | custom fusion | bytes 10488320 | tf_op jit(solution)/shard_map/jit(_take)/gather | solution.py:67
  68.1 3.4 copy.50
  71.6 1.3 broadcast_select_fusion
  72.9 3.2 copy.51
  76.1 5.2 %all-to-all-start.1 = ((bf16[2,4,160,16,128]{4,3,2,0,1:T(8,128)(2,1)}), bf16[2,4,160,16,128]{4,3,2,0,1:T(8,128)(2,1)}, u32[]{:S(2)}, u32[]{:S(2)}) async-start(bf16[2,4,160,16,128]{4,3,2,0,1:T(8,128)(2,1)} %copy.51), calls=%async_computation.1 | async-start | bytes 10485760 | tf_op jit(solution)/shard_map/all_to_all | solution.py:77
  82.4 0.3 copy.54
  83.4 24.8 %scatter_fusion = pred[4,160]{1,0:T(4,128)(4,1)S(1)} fusion(pred[4,160]{1,0:T(4,128)(4,1)S(1)} %broadcast_in_dim.163, s32[512]{0:T(512)S(1)} %bitcast.132, pred[512]{0:T(512)(128)(4,1)S(1)} %iota_compare_fusion.4), kind=kCustom, calls=%fused_computation.1 | custom fusion | bytes 5632 | tf_op jit(solution)/shard_map/scatter | solution.py:59
  108.3 1.8 fusion.14
  110.1 85.7 %all-to-all-done.1 = bf16[2,4,160,16,128]{4,3,2,0,1:T(8,128)(2,1)} async-done(((bf16[2,4,160,16,128]{4,3,2,0,1:T(8,128)(2,1)}), bf16[2,4,160,16,128]{4,3,2,0,1:T(8,128)(2,1)}, u32[]{:S(2)}, u32[]{:S(2)}) %all-to-all-start.1) | async-done | bytes 5242912 | tf_op jit(solution)/shard_map/all_to_all | solution.py:77
  195.8 118.3 %while.18 = (s32[]{:T(128)}, f32[8,256]{1,0:T(8,128)S(1)}, f32[8,256]{1,0:T(8,128)S(1)}, f32[8,256,128]{2,1,0:T(8,128)S(1)}, pred[4,160]{1,0:T(4,128)(4,1)S(1)},...) while((s32[]{:T(128)}, f32[8,256]{1,0:T(8,128)S(1)}, ...), condition=%wide.region_8.9_spmd.clone, body=%wide.region_5.8_spmd.clone.sunk | while | flops 2742822912 | bytes 156122736 | solution.py:87
  196.0 1.5 dynamic-slice_bitcast_fusion.2
  197.6 0.2 fusion.63
  197.8 9.0 %fusion.64 = (f32[8,256]{1,0:T(8,128)S(1)}, f32[2560,256,8]{1,0,2:T(8,128)}) fusion(pred[2560]{0:T(1024)(128)(4,1)S(1)} %broadcast_in_dim.232, bf16[2560,128,1]{1,0,2:T(8,128)(2,1)S(1)} %bitcast.133, bf16[256,8,128]{2,0,1:T(8,128)(2,1)S(1)} %get-tuple-element.286), kind=kOutput, calls=%fused_computation.6.clone.1 | convolution fusion | flops 1357903872 | bytes 22161920 | tf_op jit(solution)/shard_map/while/body/eval_jaxpr/thd,kd->htk/dot_general | solution.py:17
  206.8 10.5 %fusion.65 = f32[8,256]{1,0:T(8,128)S(1)} fusion(f32[2560,256,8]{1,0,2:T(8,128)} %get-tuple-element.258, f32[8,256]{1,0:T(8,128)S(1)} %select_maximum_fusion.2, pred[2560]{0:T(1024)(128)(4,1)S(1)} %broadcast_in_dim.232), kind=kLoop, calls=%fused_computation.10.clone.1 | loop fusion | flops 20969472 | bytes 20990464 | tf_op jit(solution)/shard_map/while/body/eval_jaxpr/reduce_sum | solution.py:23
  217.3 2.4 copy-done.2
  219.8 5.5 %fusion.67 = f32[8,256,128]{2,1,0:T(8,128)S(1)} fusion(bf16[2560,128,1]{1,0,2:T(8,128)(2,1)S(1)} %bitcast.136, f32[2560,256,8]{1,0,2:T(8,128)S(1)} %copy-done.2, f32[8,256]{1,0:T(8,128)S(1)} %select_maximum_fusion.2, pred[2560]{0:T(1024)(128)(4,1)S(1)} %broadcast_in_dim.232, f32[8,256,128]{2,1,0:T(8,128)S(1)} %get-tuple-element.274, ...), kind=kOutput, calls=%fused_computation.13.clone.1 | convolution fusion | flops 1363935232 | bytes 23742976 | tf_op jit(solution)/shard_map/while/body/eval_jaxpr/htk,kd->htd/dot_general | solution.py:24
  225.6 1.5 dynamic-slice_bitcast_fusion.2
  227.4 9.0 %fusion.64 = (f32[8,256]{1,0:T(8,128)S(1)}, f32[2560,256,8]{1,0,2:T(8,128)}) fusion(pred[2560]{0:T(1024)(128)(4,1)S(1)} %broadcast_in_dim.232, bf16[2560,128,1]{1,0,2:T(8,128)(2,1)S(1)} %bitcast.133, bf16[256,8,128]{2,0,1:T(8,128)(2,1)S(1)} %get-tuple-element.286), kind=kOutput, calls=%fused_computation.6.clone.1 | convolution fusion | flops 1357903872 | bytes 22161920 | tf_op jit(solution)/shard_map/while/body/eval_jaxpr/thd,kd->htk/dot_general | solution.py:17
  236.3 10.5 %fusion.65 = f32[8,256]{1,0:T(8,128)S(1)} fusion(f32[2560,256,8]{1,0,2:T(8,128)} %get-tuple-element.258, f32[8,256]{1,0:T(8,128)S(1)} %select_maximum_fusion.2, pred[2560]{0:T(1024)(128)(4,1)S(1)} %broadcast_in_dim.232), kind=kLoop, calls=%fused_computation.10.clone.1 | loop fusion | flops 20969472 | bytes 20990464 | tf_op jit(solution)/shard_map/while/body/eval_jaxpr/reduce_sum | solution.py:23
  246.9 2.4 copy-done.2
  249.3 5.5 %fusion.67 = f32[8,256,128]{2,1,0:T(8,128)S(1)} fusion(bf16[2560,128,1]{1,0,2:T(8,128)(2,1)S(1)} %bitcast.136, f32[2560,256,8]{1,0,2:T(8,128)S(1)} %copy-done.2, f32[8,256]{1,0:T(8,128)S(1)} %select_maximum_fusion.2, pred[2560]{0:T(1024)(128)(4,1)S(1)} %broadcast_in_dim.232, f32[8,256,128]{2,1,0:T(8,128)S(1)} %get-tuple-element.274, ...), kind=kOutput, calls=%fused_computation.13.clone.1 | convolution fusion | flops 1363935232 | bytes 23742976 | tf_op jit(solution)/shard_map/while/body/eval_jaxpr/htk,kd->htd/dot_general | solution.py:24
  255.1 1.5 dynamic-slice_bitcast_fusion.2
  256.9 9.0 %fusion.64 = (f32[8,256]{1,0:T(8,128)S(1)}, f32[2560,256,8]{1,0,2:T(8,128)}) fusion(pred[2560]{0:T(1024)(128)(4,1)S(1)} %broadcast_in_dim.232, bf16[2560,128,1]{1,0,2:T(8,128)(2,1)S(1)} %bitcast.133, bf16[256,8,128]{2,0,1:T(8,128)(2,1)S(1)} %get-tuple-element.286), kind=kOutput, calls=%fused_computation.6.clone.1 | convolution fusion | flops 1357903872 | bytes 22161920 | tf_op jit(solution)/shard_map/while/body/eval_jaxpr/thd,kd->htk/dot_general | solution.py:17
  265.8 10.5 %fusion.65 = f32[8,256]{1,0:T(8,128)S(1)} fusion(f32[2560,256,8]{1,0,2:T(8,128)} %get-tuple-element.258, f32[8,256]{1,0:T(8,128)S(1)} %select_maximum_fusion.2, pred[2560]{0:T(1024)(128)(4,1)S(1)} %broadcast_in_dim.232), kind=kLoop, calls=%fused_computation.10.clone.1 | loop fusion | flops 20969472 | bytes 20990464 | tf_op jit(solution)/shard_map/while/body/eval_jaxpr/reduce_sum | solution.py:23
  276.4 2.4 copy-done.2
  278.8 5.5 %fusion.67 = f32[8,256,128]{2,1,0:T(8,128)S(1)} fusion(bf16[2560,128,1]{1,0,2:T(8,128)(2,1)S(1)} %bitcast.136, f32[2560,256,8]{1,0,2:T(8,128)S(1)} %copy-done.2, f32[8,256]{1,0:T(8,128)S(1)} %select_maximum_fusion.2, pred[2560]{0:T(1024)(128)(4,1)S(1)} %broadcast_in_dim.232, f32[8,256,128]{2,1,0:T(8,128)S(1)} %get-tuple-element.274, ...), kind=kOutput, calls=%fused_computation.13.clone.1 | convolution fusion | flops 1363935232 | bytes 23742976 | tf_op jit(solution)/shard_map/while/body/eval_jaxpr/htk,kd->htd/dot_general | solution.py:24
  284.6 1.5 dynamic-slice_bitcast_fusion.2
  286.4 9.0 %fusion.64 = (f32[8,256]{1,0:T(8,128)S(1)}, f32[2560,256,8]{1,0,2:T(8,128)}) fusion(pred[2560]{0:T(1024)(128)(4,1)S(1)} %broadcast_in_dim.232, bf16[2560,128,1]{1,0,2:T(8,128)(2,1)S(1)} %bitcast.133, bf16[256,8,128]{2,0,1:T(8,128)(2,1)S(1)} %get-tuple-element.286), kind=kOutput, calls=%fused_computation.6.clone.1 | convolution fusion | flops 1357903872 | bytes 22161920 | tf_op jit(solution)/shard_map/while/body/eval_jaxpr/thd,kd->htk/dot_general | solution.py:17
  295.4 10.5 %fusion.65 = f32[8,256]{1,0:T(8,128)S(1)} fusion(f32[2560,256,8]{1,0,2:T(8,128)} %get-tuple-element.258, f32[8,256]{1,0:T(8,128)S(1)} %select_maximum_fusion.2, pred[2560]{0:T(1024)(128)(4,1)S(1)} %broadcast_in_dim.232), kind=kLoop, calls=%fused_computation.10.clone.1 | loop fusion | flops 20969472 | bytes 20990464 | tf_op jit(solution)/shard_map/while/body/eval_jaxpr/reduce_sum | solution.py:23
  305.9 2.4 copy-done.2
  308.4 5.5 %fusion.67 = f32[8,256,128]{2,1,0:T(8,128)S(1)} fusion(bf16[2560,128,1]{1,0,2:T(8,128)(2,1)S(1)} %bitcast.136, f32[2560,256,8]{1,0,2:T(8,128)S(1)} %copy-done.2, f32[8,256]{1,0:T(8,128)S(1)} %select_maximum_fusion.2, pred[2560]{0:T(1024)(128)(4,1)S(1)} %broadcast_in_dim.232, f32[8,256,128]{2,1,0:T(8,128)S(1)} %get-tuple-element.274, ...), kind=kOutput, calls=%fused_computation.13.clone.1 | convolution fusion | flops 1363935232 | bytes 23742976 | tf_op jit(solution)/shard_map/while/body/eval_jaxpr/htk,kd->htd/dot_general | solution.py:24
  314.1 0.3 copy.56
  314.5 2.0 fusion.17
  316.5 2.2 fusion.20
  318.7 7.3 %convolution_convert_fusion = bf16[256,4096]{1,0:T(8,128)(2,1)} fusion(bf16[256,1024]{0,1:T(8,128)(2,1)S(1)} %bitcast.139, bf16[1024,4096]{1,0:T(8,128)(2,1)} %param.14), kind=kOutput, calls=%fused_computation.24 | convolution fusion | flops 2148532224 | bytes 11010048 | tf_op jit(solution)/shard_map/dot_general | solution.py:101
  326.5 1.4 scatter_fusion.2
  327.9 0.7 copy.60
  328.7 3.4 all-to-all-start.2
  332.1 8.3 %all-to-all-done.2 = bf16[2,4,8,16,128]{4,3,2,0,1:T(8,128)(2,1)S(1)} async-done(((bf16[2,4,8,16,128]{4,3,2,0,1:T(8,128)(2,1)}), bf16[2,4,8,16,128]{4,3,2,0,1:T(8,128)(2,1)S(1)}, u32[]{:S(2)}, u32[]{:S(2)}) %all-to-all-start.2) | async-done | bytes 262176 | tf_op jit(solution)/shard_map/all_to_all | solution.py:121
  340.4 0.7 copy.61
  341.1 15.6 %reduce-scatter.2.cloned.1.call-done = bf16[64,4096]{1,0:T(8,128)(2,1)} async-done(((bf16[256,4096]{1,0:T(8,128)(2,1)}), bf16[64,4096]{1,0:T(8,128)(2,1)}) %reduce-scatter.2.cloned.1.call-update) | async-done | bytes 524304 | tf_op jit(solution)/shard_map/reduce_scatter | solution.py:100
  356.7 2.0 select_convert_fusion
  (71 shorter events, 3.3 us)
Async XLA Ops:
  7.2 56.9 %copy-start = (bf16[2,256,16,128]{3,2,1,0:T(8,128)(2,1)S(1)}, bf16[2,256,16,128]{3,2,1,0:T(8,128)(2,1)}, u32[]{:S(2)}) copy-start(bf16[2,256,16,128]{3,2,1,0:T(8,128)(2,1)} %param.12) | copy-start | bytes 6291460
  76.1 6.1 %copy-start.3 = (bf16[256,1024]{1,0:T(8,128)(2,1)S(1)}, bf16[256,1024]{1,0:T(8,128)(2,1)}, u32[]{:S(2)}) copy-start(bf16[256,1024]{1,0:T(8,128)(2,1)} %param.11) | copy-start | bytes 1572868
  76.1 32.2 %copy-start.4 = (bf16[2,256,128]{2,1,0:T(8,128)(2,1)S(1)}, bf16[2,256,128]{2,1,0:T(8,128)(2,1)}, u32[]{:S(2)}) copy-start(bf16[2,256,128]{2,1,0:T(8,128)(2,1)} %param.13) | copy-start | bytes 393220
  76.1 119.7 %all-to-all-start.1 = ((bf16[2,4,160,16,128]{4,3,2,0,1:T(8,128)(2,1)}), bf16[2,4,160,16,128]{4,3,2,0,1:T(8,128)(2,1)}, u32[]{:S(2)}, u32[]{:S(2)}) async-start(bf16[2,4,160,16,128]{4,3,2,0,1:T(8,128)(2,1)} %copy.51), calls=%async_computation.1 | async-start | bytes 10485760 | tf_op jit(solution)/shard_map/all_to_all | solution.py:77
  81.3 275.4 %reduce-scatter.2.cloned.1.call-start = ((), (), s32[]{:S(2)}) async-start(), calls=%async_computation.4 | async-start | bytes 2621440 | tf_op jit(solution)/shard_map/reduce_scatter | solution.py:100
  206.8 13.0 %copy-start.2 = (f32[2560,256,8]{1,0,2:T(8,128)S(1)}, f32[2560,256,8]{1,0,2:T(8,128)}, u32[]{:S(2)}) copy-start(f32[2560,256,8]{1,0,2:T(8,128)} %get-tuple-element.258) | copy-start | bytes 62914564 | tf_op jit(solution)/shard_map/while
  236.3 13.0 %copy-start.2 = (f32[2560,256,8]{1,0,2:T(8,128)S(1)}, f32[2560,256,8]{1,0,2:T(8,128)}, u32[]{:S(2)}) copy-start(f32[2560,256,8]{1,0,2:T(8,128)} %get-tuple-element.258) | copy-start | bytes 62914564 | tf_op jit(solution)/shard_map/while
  265.8 13.0 %copy-start.2 = (f32[2560,256,8]{1,0,2:T(8,128)S(1)}, f32[2560,256,8]{1,0,2:T(8,128)}, u32[]{:S(2)}) copy-start(f32[2560,256,8]{1,0,2:T(8,128)} %get-tuple-element.258) | copy-start | bytes 62914564 | tf_op jit(solution)/shard_map/while
  295.4 13.0 %copy-start.2 = (f32[2560,256,8]{1,0,2:T(8,128)S(1)}, f32[2560,256,8]{1,0,2:T(8,128)}, u32[]{:S(2)}) copy-start(f32[2560,256,8]{1,0,2:T(8,128)} %get-tuple-element.258) | copy-start | bytes 62914564 | tf_op jit(solution)/shard_map/while
  318.7 7.4 %copy-start.5 = (s32[1,16,1]{1,2,0:T(1,128)S(1)}, s32[1,16,1]{1,2,0:T(1,128)}, u32[]{:S(2)}) copy-start(s32[1,16,1]{1,2,0:T(1,128)} %param.19) | copy-start | bytes 196
  318.7 40.0 %copy-start.1 = (bf16[2,256,16,128]{3,2,1,0:T(8,128)(2,1)S(1)}, bf16[2,256,16,128]{3,2,1,0:T(8,128)(2,1)}, u32[]{:S(2)}) copy-start(bf16[2,256,16,128]{3,2,1,0:T(8,128)(2,1)} %param.12) | copy-start | bytes 6291460
  328.7 11.7 %all-to-all-start.2 = ((bf16[2,4,8,16,128]{4,3,2,0,1:T(8,128)(2,1)}), bf16[2,4,8,16,128]{4,3,2,0,1:T(8,128)(2,1)S(1)}, u32[]{:S(2)}, u32[]{:S(2)}) async-start(bf16[2,4,8,16,128]{4,3,2,0,1:T(8,128)(2,1)} %copy.60), calls=%async_computation.3 | async-start | bytes 524288 | tf_op jit(solution)/shard_map/all_to_all | solution.py:121
Sparse Core Ops, SparseCore 0:
  326.1 30.5 reduce-scatter.1
where the time goes:
time: 368 us; the launch traced here: 366 us
  waiting for transfers between devices  110 us (30%)
  local copies, waits for them, and re-layouts  99.8 us (27%)
  matrix products  69.1 us (19%)
  other arithmetic  51.9 us (14%)
  between operations  15.6 us (4%)
  blocking collectives  10.2 us (3%)
  starting transfers between devices  8.8 us (2%)
    all_to_all x1, waiting for transfers between devices, shards(): lax.all_to_all(picked, 'inst', split_axis=1, concat_axis=1, tiled=True)  85.7 us
    reduce_sum x5, other arithmetic, absorb(): running_sum = running_sum * rescale + jnp.sum(weights, axis=-1)  44.2 us
    scatter x1, local copies, waits for them, and re-layouts, shards(): wanted = jnp.zeros((peer_count, cap_pad), jnp.int32).at[clamped, place].s...  42.5 us
    dot_general x5, matrix products, absorb(): jnp.einsum('thd,kd->htk', query_heads, key_rows, preferred_element_type=j...  37.6 us
    scatter x1, local copies, waits for them, and re-layouts, shards(): jnp.zeros((peer_count, cap_pad), bool).at[clamped, place]  24.8 us
    dot_general x5, matrix products, absorb(): jnp.einsum('htk,kd->htd', weights.astype(jnp.bfloat16), value_rows, prefe...  24.2 us
    reduce_scatter x1, waiting for transfers between devices, shards(): lax.psum_scatter(jnp.dot(attended, out_weight, preferred_element_type=jnp...  15.6 us
    all_to_all x1, blocking collectives, shards(): lax.all_to_all(wanted, 'inst', split_axis=0, concat_axis=0, tiled=True)  10.2 us
  transfers between devices with their start and end apart: 3, of which 3 were waited for; matrix products, arithmetic and copies ran while one was open for 8% of the time, Pallas kernels for 0%

commit v1 on v0

v1 whole, which is shorter than its diff:
```python
import functools
import math

import jax
import jax.numpy as jnp
from jax import lax
from jax.experimental import pallas as pl
from jax.experimental.pallas import tpu as pltpu
from jax.sharding import PartitionSpec as P

LOW = -1e30
TILE = 16
VMEM_LIMIT = 48 * 1024 * 1024

SMEM = pl.BlockSpec(memory_space=pltpu.SMEM)
VMEM = pl.BlockSpec(memory_space=pltpu.VMEM)


def round_up(number, step):
    return -(-number // step) * step


def route_kernel(peers, me_ref, live_ref, holders_ref, slots_ref, lists_ref):
    last = lists_ref.shape[1] - 1
    me = me_ref[0]
    for k in range(peers):
        lists_ref[k, last] = 0

    def step(j, carry):
        away = holders_ref[j] - me
        away = jnp.where(away < 0, away + peers, away)
        count = lists_ref[away, last]
        lists_ref[away, count] = slots_ref[j]
        lists_ref[away, last] = count + 1
        return carry

    lax.fori_loop(0, live_ref[0], step, 0)


def route(me, live, holders, slots, peers, cap):
    width = round_up(cap + 1, 128)
    return pl.pallas_call(
        functools.partial(route_kernel, peers),
        out_shape=jax.ShapeDtypeStruct((peers, width), jnp.int32),
        in_specs=[SMEM] * 4,
        out_specs=SMEM,
        name="route",
    )(me, live, holders, slots)


def absorb_tile(keys, values_ref, q_ref, max_ref, acc_ref, scale, mask=None):
    heads, _, rows = max_ref.shape
    head_dim = keys.shape[1]
    values = values_ref[...]
    for g in range(heads):
        q = q_ref[:, g * head_dim : (g + 1) * head_dim]
        s = lax.dot_general(
            keys, q, (((1,), (1,)), ((), ())), preferred_element_type=jnp.float32
        )
        if mask is not None:
            s = jnp.where(mask, s, LOW)
        old = max_ref[g]
        new = jnp.maximum(old, jnp.max(s, axis=0, keepdims=True))
        p = jnp.exp2((s - new) * scale).astype(jnp.bfloat16)
        update = jnp.dot(values, p, preferred_element_type=jnp.float32)
        acc_ref[g] = acc_ref[g] * jnp.exp2((old - new) * scale) + update
        max_ref[g] = new


def put_values(values, valid_keys, vt_ref):
    head_dim = values.shape[1]
    keys = values.shape[0]
    vt_ref[:head_dim, :] = values.T
    row = lax.broadcasted_iota(jnp.int32, (16, keys), 0)
    col = lax.broadcasted_iota(jnp.int32, (16, keys), 1)
    vt_ref[head_dim:, :] = jnp.where((row == 0) & (col < valid_keys), 1.0, 0.0).astype(
        jnp.bfloat16
    )


def absorb_blocks(list_ref, q_ref, store_ref, k_ref, v_ref, vt_ref, max_ref, acc_ref, scale):
    block_rows = store_ref.shape[2]
    count = list_ref[list_ref.shape[0] - 1]

    def step(tile, carry):
        for j in range(TILE):
            index = tile * TILE + j
            slot = list_ref[jnp.minimum(index, count - 1)]
            k_ref[j * block_rows : (j + 1) * block_rows, :] = store_ref[0, slot]
            block = store_ref[1, slot]
            v_ref[j * block_rows : (j + 1) * block_rows, :] = jnp.where(
                index < count, block, jnp.zeros_like(block)
            )
        put_values(v_ref[...], (count - tile * TILE) * block_rows, vt_ref)
        absorb_tile(k_ref[...], vt_ref, q_ref, max_ref, acc_ref, scale)
        return carry

    lax.fori_loop(0, (count + TILE - 1) // TILE, step, 0)


def reset(max_ref, acc_ref):
    max_ref[...] = jnp.full_like(max_ref, LOW)
    acc_ref[...] = jnp.zeros_like(acc_ref)


def finish(out_ref, max_ref, acc_ref, scale):
    heads, _, rows = max_ref.shape
    head_dim = acc_ref.shape[1] - 16
    logs = []
    for g in range(heads):
        total = acc_ref[g, head_dim : head_dim + 8, :][:1]
        some = total > 0.0
        inverse = jnp.where(some, 1.0 / jnp.where(some, total, 1.0), 0.0)
        out_ref[g * head_dim : (g + 1) * head_dim, :] = (
            acc_ref[g, :head_dim, :] * inverse
        ).astype(jnp.bfloat16)
        logs.append(
            jnp.where(some, max_ref[g] * scale + jnp.log2(jnp.where(some, total, 1.0)), LOW)
        )
    logs = jnp.concatenate(logs, axis=0)
    first = logs.astype(jnp.bfloat16).astype(jnp.float32)
    rest = logs - first
    second = rest.astype(jnp.bfloat16).astype(jnp.float32)
    third = rest - second
    pieces = jnp.concatenate([first, second, third, jnp.zeros_like(first)], axis=0)
    out_ref[heads * head_dim :, :] = pieces.astype(jnp.bfloat16)


def own_kernel(
    scale, span_live_ref, list_ref, q_ref, store_ref, span_ref, out_ref,
    k_ref, v_ref, vt_ref, max_ref, acc_ref,
):
    reset(max_ref, acc_ref)
    rows = q_ref.shape[0]
    keys = span_ref.shape[1]
    key = lax.broadcasted_iota(jnp.int32, (keys, rows), 0)
    row = lax.broadcasted_iota(jnp.int32, (keys, rows), 1)
    put_values(span_ref[1], keys, vt_ref)
    absorb_tile(
        span_ref[0], vt_ref, q_ref, max_ref, acc_ref, scale,
        (key <= row) & (key < span_live_ref[0]),
    )
    absorb_blocks(list_ref, q_ref, store_ref, k_ref, v_ref, vt_ref, max_ref, acc_ref, scale)
    finish(out_ref, max_ref, acc_ref, scale)


def guest_kernel(
    scale, list_a_ref, list_b_ref, q_a_ref, q_b_ref, store_ref, out_a_ref, out_b_ref,
    k_ref, v_ref, vt_ref, max_ref, acc_ref,
):
    for list_ref, q_ref, out_ref in (
        (list_a_ref, q_a_ref, out_a_ref),
        (list_b_ref, q_b_ref, out_b_ref),
    ):
        reset(max_ref, acc_ref)
        absorb_blocks(list_ref, q_ref, store_ref, k_ref, v_ref, vt_ref, max_ref, acc_ref, scale)
        finish(out_ref, max_ref, acc_ref, scale)


def attention_scratch(heads, rows, head_dim, block_rows):
    keys = TILE * block_rows
    return [
        pltpu.VMEM((keys, head_dim), jnp.bfloat16),
        pltpu.VMEM((keys, head_dim), jnp.bfloat16),
        pltpu.VMEM((head_dim + 16, keys), jnp.bfloat16),
        pltpu.VMEM((heads, 1, rows), jnp.float32),
        pltpu.VMEM((heads, head_dim + 16, rows), jnp.float32),
    ]


def attention_cost(rows, keys, head_dim, heads):
    return pl.CostEstimate(
        flops=4 * rows * keys * head_dim * heads,
        bytes_accessed=4 * 1024 * 1024,
        transcendentals=rows * keys * heads,
    )


def project_kernel(
    peers, me_ref, span_live_ref, *refs
):
    parts = refs[: 2 * peers - 1]
    weight_ref, out_ref, att_ref = refs[2 * peers - 1 :]
    rows, features = att_ref.shape

    @pl.when(pl.program_id(0) == 0)
    def _():
        heads = 8 * ((parts[0].shape[0] - features) // 32)
        head_dim = features // heads
        me = me_ref[0]
        logs = []
        for index, part in enumerate(parts):
            pieces = part[features:, :].astype(jnp.float32)
            log = pieces[:heads] + pieces[heads : 2 * heads] + pieces[2 * heads : 3 * heads]
            if index:
                away = (index + 1) // 2
                valid = me >= away if index % 2 else me + away < peers
                log = jnp.where(valid, log, LOW)
            logs.append(log)
        top = functools.reduce(jnp.maximum, logs)
        weights = [jnp.exp2(log - top) for log in logs]
        inverse = 1.0 / functools.reduce(jnp.add, weights)
        row = lax.broadcasted_iota(jnp.int32, (heads, rows), 1)
        inverse = jnp.where(row < span_live_ref[0], inverse, 0.0)
        weights = [weight * inverse for weight in weights]
        for g in range(heads):
            total = jnp.zeros((head_dim, rows), jnp.float32)
            for part, weight in zip(parts, weights):
                total += part[g * head_dim : (g + 1) * head_dim, :].astype(jnp.float32) * weight[
                    g : g + 1
                ]
            att_ref[:, g * head_dim : (g + 1) * head_dim] = total.T.astype(jnp.bfloat16)

    out_ref[...] = jnp.dot(
        att_ref[...], weight_ref[...], preferred_element_type=jnp.float32
    ).astype(jnp.bfloat16)


def project(me, span_live, parts, out_weight, peers):
    features, outputs = out_weight.shape
    rows = parts[0].shape[1]
    width = 512
    whole = lambda i, *_: (0, 0)
    return pl.pallas_call(
        functools.partial(project_kernel, peers),
        out_shape=jax.ShapeDtypeStruct((rows, outputs), jnp.bfloat16),
        grid_spec=pltpu.PrefetchScalarGridSpec(
            num_scalar_prefetch=2,
            grid=(outputs // width,),
            in_specs=[pl.BlockSpec(part.shape, whole) for part in parts]
            + [pl.BlockSpec((features, width), lambda i, *_: (0, i))],
            out_specs=pl.BlockSpec((rows, width), lambda i, *_: (0, i)),
            scratch_shapes=[pltpu.VMEM((rows, features), jnp.bfloat16)],
        ),
        compiler_params=pltpu.CompilerParams(vmem_limit_bytes=VMEM_LIMIT),
        cost_estimate=pl.CostEstimate(
            flops=2 * rows * features * outputs,
            bytes_accessed=2 * (features + rows) * outputs,
            transcendentals=0,
        ),
        name="project",
    )(me, span_live, *parts, out_weight)


def pack_kernel(span_live_ref, owners_ref, span_ref, out_ref, counts_ref):
    peers = out_ref.shape[1]
    block_rows, head_dim = out_ref.shape[3:]
    out_ref[...] = jnp.zeros_like(out_ref)
    for k in range(peers):
        counts_ref[k] = 0
    row = lax.broadcasted_iota(jnp.int32, (block_rows, head_dim), 0)
    for b in range(span_ref.shape[1] // block_rows):
        owner = owners_ref[b]
        rank = counts_ref[owner]
        counts_ref[owner] = rank + 1
        keep = row + b * block_rows < span_live_ref[0]
        for side in range(2):
            block = span_ref[side, b * block_rows : (b + 1) * block_rows, :]
            out_ref[side, owner, rank] = jnp.where(keep, block, jnp.zeros_like(block))


def shards(
    queries,
    cache_store,
    span_cache,
    out_weight,
    prefix_blocks,
    span_lengths,
    hit_holders,
    hit_slots,
    store_owners,
):
    peers = lax.axis_size("inst")
    block_rows, head_dim = cache_store.shape[2:]
    rows = queries.shape[0]
    heads = queries.shape[1] // head_dim
    block_max = hit_slots.shape[1]
    cap = max(2, block_max * 5 // (4 * peers))
    new_count = rows // block_rows
    push_cap = max(2, 2 * new_count // peers)
    scale = math.log2(math.e) / math.sqrt(head_dim)
    me = lax.axis_index("inst").reshape(1)
    part_shape = jax.ShapeDtypeStruct((heads * head_dim + 4 * heads, rows), jnp.bfloat16)

    def shift(value, by):
        pairs = [(i, i + by) for i in range(peers) if 0 <= i + by < peers]
        return lax.ppermute(value, "inst", pairs)

    lists = route(me, prefix_blocks, hit_holders.reshape(-1), hit_slots.reshape(-1), peers, cap)

    from_left, from_right = [queries], [queries]
    for away in range(1, peers):
        from_left.append(shift(from_left[-1], 1))
        from_right.append(shift(from_right[-1], -1))

    own = pl.pallas_call(
        functools.partial(own_kernel, scale),
        out_shape=part_shape,
        in_specs=[SMEM, SMEM, VMEM, VMEM, VMEM],
        out_specs=VMEM,
        scratch_shapes=attention_scratch(heads, rows, head_dim, block_rows),
        compiler_params=pltpu.CompilerParams(vmem_limit_bytes=VMEM_LIMIT),
        cost_estimate=attention_cost(rows, 4 * rows, head_dim, heads),
        name="own_attention",
    )(span_lengths, lists[0], queries, cache_store, span_cache)

    parts = [own]
    for away in range(1, peers):
        list_a = shift(lists[away], away)
        list_b = shift(lists[peers - away], -away)
        part_a, part_b = pl.pallas_call(
            functools.partial(guest_kernel, scale),
            out_shape=(part_shape, part_shape),
            in_specs=[SMEM, SMEM, VMEM, VMEM, VMEM],
            out_specs=(VMEM, VMEM),
            scratch_shapes=attention_scratch(heads, rows, head_dim, block_rows),
            compiler_params=pltpu.CompilerParams(vmem_limit_bytes=VMEM_LIMIT),
            cost_estimate=attention_cost(rows, 6 * rows, head_dim, heads),
            name="guest_attention",
        )(list_a, list_b, from_left[away], from_right[away], cache_store)
        parts.append(shift(part_b, away))
        parts.append(shift(part_a, -away))

    partial = project(me, span_lengths, parts, out_weight, peers)
    projected = lax.psum_scatter(partial, "tp", scatter_dimension=0, tiled=True)

    outgoing = pl.pallas_call(
        pack_kernel,
        out_shape=jax.ShapeDtypeStruct(
            (2, peers, push_cap, block_rows, head_dim), jnp.bfloat16
        ),
        in_specs=[SMEM, SMEM, VMEM],
        out_specs=VMEM,
        scratch_shapes=[pltpu.SMEM((peers,), jnp.int32)],
        compiler_params=pltpu.CompilerParams(vmem_limit_bytes=VMEM_LIMIT),
        name="pack_blocks",
    )(span_lengths, store_owners.reshape(-1), span_cache)
    incoming = lax.all_to_all(outgoing, "inst", split_axis=1, concat_axis=1, tiled=True)
    pushed_blocks = incoming.reshape(2, peers * push_cap, block_rows, head_dim)
    return (projected, pushed_blocks)


def solution(mesh):
    return jax.shard_map(
        shards,
        mesh=mesh,
        in_specs=(
            P(("pods", "inst"), "tp"),
            P(None, ("pods", "inst"), None, "tp"),
            P(None, ("pods", "inst"), "tp"),
            P("tp", None),
            P(("pods", "inst")),
            P(("pods", "inst")),
            P(("pods", "inst"), None, None),
            P(("pods", "inst"), None),
            P(("pods", "inst"), None, None),
        ),
        out_specs=(P(("pods", "inst", "tp"), None), P(None, ("pods", "inst"), None, "tp")),
        check_vma=False,
    )
```

time: 368 us -> 238 us (0.65)
  local copies, waits for them, and re-layouts: 99.8 us -> 3.82 us
  Pallas kernels: 0 us -> 85 us
  waiting for transfers between devices: 110 us -> 29.2 us
  starting transfers between devices: 8.8 us -> 82.4 us
  matrix products: 69.1 us -> 0 us
  other arithmetic: 51.9 us -> 0 us
  blocking collectives: 10.2 us -> 22.2 us
    all_to_all x2 -> x0, waiting for transfers between devices: 94 us -> none  [the longest x1 85.7 us: shards(): lax.all_to_all(picked, 'inst', split_axis=1, concat_axis=1, tiled=True)]
    pallas_call x0 -> x7, Pallas kernels: none -> 85 us  [the longest x3 58.2 us: shards(): pl.pallas_call(functools.partial(guest_kernel, scale), out_shape=(part_sh...]
    ppermute x0 -> x18, starting transfers between devices: none -> 82.3 us  [shift(): return lax.ppermute(value, 'inst', pairs)]
    scatter x4 -> x0, local copies, waits for them, and re-layouts: 69.5 us -> none  [the longest x1 42.5 us: shards(): wanted = jnp.zeros((peer_count, cap_pad), jnp.int32).at[clamped, place].s...]
    dot_general x11 -> x0, matrix products: 69.1 us -> none  [the longest x5 37.6 us: absorb(): jnp.einsum('thd,kd->htk', query_heads, key_rows, preferred_element_type=j...]
    reduce_sum x7 -> x0, other arithmetic: 45 us -> none  [the longest x5 44.2 us: absorb(): running_sum = running_sum * rescale + jnp.sum(weights, axis=-1)]
    all_to_all x1, blocking collectives: 10.2 us -> 22.2 us  [shards(): lax.all_to_all(outgoing, 'inst', split_axis=1, concat_axis=1, tiled=True)]
    ppermute x0 -> x18, waiting for transfers between devices: none -> 10.2 us  [shift(): return lax.ppermute(value, 'inst', pairs)]
  transfers between devices with their start and end apart: 3 -> 19, of which waited for: 3 -> 2; matrix products, arithmetic and copies ran while one was open for 8% -> 1% of each run, Pallas kernels for 0% -> 32%
where the time goes in v1:
time: 238 us
  Pallas kernels  85 us (36%)
  starting transfers between devices  82.4 us (35%)
  waiting for transfers between devices  29.2 us (12%)
  blocking collectives  22.2 us (9%)
  between operations  15.7 us (7%)
  local copies, waits for them, and re-layouts  3.82 us (2%)
    ppermute x18, starting transfers between devices, shift(): return lax.ppermute(value, 'inst', pairs)  82.3 us
    pallas_call x3, Pallas kernels, shards(): pl.pallas_call(functools.partial(guest_kernel, scale), out_shape=(part_sh...  58.2 us
    all_to_all x1, blocking collectives, shards(): lax.all_to_all(outgoing, 'inst', split_axis=1, concat_axis=1, tiled=True)  22.2 us
    reduce_scatter x1, waiting for transfers between devices, shards(): projected = lax.psum_scatter(partial, 'tp', scatter_dimension=0, tiled=True)  19 us
    pallas_call x1, Pallas kernels, shards(): pl.pallas_call(functools.partial(own_kernel, scale), out_shape=part_shape...  12.8 us
    ppermute x18, waiting for transfers between devices, shift(): return lax.ppermute(value, 'inst', pairs)  10.2 us
    pallas_call x1, Pallas kernels, project(): pl.pallas_call(functools.partial(project_kernel, peers), out_shape=jax.Sh...  9.46 us
  transfers between devices with their start and end apart: 19, of which 2 were waited for; matrix products, arithmetic and copies ran while one was open for 1% of the time, Pallas kernels for 32%

profile of v1, /device:TPU:4, one launch (start us, length us, event | category | flops | bytes accessed | tf_op | source)
XLA Modules:
  0.0 238.3 jit_solution(15806738305517362972)
XLA Ops:
  7.2 0.0 reduce-scatter.2.cloned.1.call-start
  7.2 3.5 %collective-permute-start.2 = (bf16[256,1024]{1,0:T(8,128)(2,1)}, bf16[256,1024]{1,0:T(8,128)(2,1)S(1)}, u32[]{:S(2)}, u32[]{:S(2)}) collective-permute-start(bf16[256,1024]{1,0:T(8,128)(2,1)} %q_ref.1), channel_id=1, source_target_pairs={{0,4},{4,8},{8,12},{1,5},{5,9},{9,13},{2,6},{6,10},{10,14},{3,7},{... | collective-permute-start | bytes 1572872 | tf_op jit(solution)/shard_map/ppermute | solution.py:287
  10.7 1.3 collective-permute-start.3
  12.0 10.1 %collective-permute-done.2.q_a_ref = bf16[256,1024]{1,0:T(8,128)(2,1)S(1)} collective-permute-done((bf16[256,1024]{1,0:T(8,128)(2,1)}, bf16[256,1024]{1,0:T(8,128)(2,1)S(1)}, u32[]{:S(2)}, u32[]{:S(2)}) %collective-permute-start.2) | collective-permute-done | bytes 524320 | tf_op jit(solution)/shard_map/ppermute | solution.py:287
  22.2 4.3 %collective-permute-start.8 = (bf16[256,1024]{1,0:T(8,128)(2,1)S(1)}, bf16[256,1024]{1,0:T(8,128)(2,1)S(1)}, u32[]{:S(2)}, u32[]{:S(2)}) collective-permute-start(bf16[256,1024]{1,0:T(8,128)(2,1)S(1)} %collective-permute-done.2.q_a_ref), channel_id=1, source_target_pairs={{0,4},{4,8},{8,12},{1,5},{5,9},{9,13},{2,6},{6,10},{10,14},{3,7},{... | collective-permute-start | bytes 1572872 | tf_op jit(solution)/shard_map/ppermute | solution.py:287
  26.5 0.0 collective-permute-done.3.q_b_ref
  26.5 1.3 collective-permute-start.9
  28.4 3.9 %route.1 = s32[4,256]{1,0:T(4,128)} custom-call(s32[1]{0:T(128)} %bitcast.me_ref, s32[1]{0:T(128)S(6)} %copy.14.live_ref, s32[512]{0:T(512)} %bitcast.12, s32[512]{0:T(512)} %bitcast.13), custom_call_target="tpu_custom_call" | custom-call | tf_op jit(solution)/shard_map/route/pallas_call | solution.py:42
  32.4 0.8 fusion
  33.2 9.1 %collective-permute-start = (s32[256]{0:T(256)S(1)}, s32[256]{0:T(256)S(1)}, u32[]{:S(2)}, u32[]{:S(2)}) collective-permute-start(s32[256]{0:T(256)S(1)} %bitcast.14), channel_id=1, source_target_pairs={{0,4},{4,8},{8,12},{1,5},{5,9},{9,13},{2,6},{6,10},{10,14},{3,7},{... | collective-permute-start | bytes 3080 | tf_op jit(solution)/shard_map/ppermute | solution.py:287
  42.3 1.3 collective-permute-start.1
  43.6 0.0 collective-permute-done.8.q_a_ref
  43.6 4.6 %collective-permute-start.14 = (bf16[256,1024]{1,0:T(8,128)(2,1)S(1)}, bf16[256,1024]{1,0:T(8,128)(2,1)S(1)}, u32[]{:S(2)}, u32[]{:S(2)}) collective-permute-start(bf16[256,1024]{1,0:T(8,128)(2,1)S(1)} %collective-permute-done.8.q_a_ref), channel_id=1, source_target_pairs={{0,4},{4,8},{8,12},{1,5},{5,9},{9,13},{2,6},{6,10},{10,14},{3,7},{... | collective-permute-start | bytes 1572872 | tf_op jit(solution)/shard_map/ppermute | solution.py:287
  48.2 0.0 collective-permute-done.9.q_b_ref
  48.2 1.3 collective-permute-start.15
  49.5 0.0 collective-permute-done.list_a_ref
  49.5 0.0 collective-permute-done.1.list_b_ref
  49.5 0.0 copy-start.2
  49.5 1.6 copy-done.2
  51.1 22.5 %guest_attention.3 = (bf16[1056,256]{1,0:T(8,128)(2,1)S(1)}, bf16[1056,256]{1,0:T(8,128)(2,1)S(1)}) custom-call(s32[256]{0:T(256)S(1)} %collective-permute-done.list_a_ref, s32[256]{0:T(256)S(1)} %collective-permute-done.1.list_b_ref, bf16[256,1024]{1,0:T(8,128)(2,1)S(1)} %collective-permute-done.2.q_a_ref, ...), custom_call_target="tpu_custom_call" | custom-call | flops 1610612736 | bytes 4194304 | tf_op jit(solution)/shard_map/guest_attention/pallas_call | solution.py:311
  73.6 1.3 collective-permute-start.4
  75.0 33.1 %collective-permute-start.6 = (s32[256]{0:T(256)S(1)}, s32[256]{0:T(256)S(1)}, u32[]{:S(2)}, u32[]{:S(2)}) collective-permute-start(s32[256]{0:T(256)S(1)} %bitcast.18), channel_id=1, source_target_pairs={{0,8},{4,12},{1,9},{5,13},{2,10},{6,14},{3,11},{7,15},{16,24},{20,... | collective-permute-start | bytes 3080 | tf_op jit(solution)/shard_map/ppermute | solution.py:287
  108.1 1.3 collective-permute-start.7
  109.4 0.0 collective-permute-done.6.list_a_ref
  109.4 11.3 %collective-permute-start.12 = (s32[256]{0:T(256)S(1)}, s32[256]{0:T(256)S(1)}, u32[]{:S(2)}, u32[]{:S(2)}) collective-permute-start(s32[256]{0:T(256)S(1)} %bitcast.17), channel_id=1, source_target_pairs={{0,12},{1,13},{2,14},{3,15},{16,28},{17,29},{18,30},{19,31}} | collective-permute-start | bytes 3080 | tf_op jit(solution)/shard_map/ppermute | solution.py:287
  120.7 0.0 collective-permute-done.7.list_b_ref
  120.7 1.3 collective-permute-start.13
  122.0 10.5 %guest_attention.4 = (bf16[1056,256]{1,0:T(8,128)(2,1)S(1)}, bf16[1056,256]{1,0:T(8,128)(2,1)S(1)}) custom-call(s32[256]{0:T(256)S(1)} %collective-permute-done.6.list_a_ref, s32[256]{0:T(256)S(1)} %collective-permute-done.7.list_b_ref, bf16[256,1024]{1,0:T(8,128)(2,1)S(1)} %collective-permute-done.8.q_a_ref, ...), custom_call_target="tpu_custom_call" | custom-call | flops 1610612736 | bytes 4194304 | tf_op jit(solution)/shard_map/guest_attention/pallas_call | solution.py:311
  132.5 0.0 collective-permute-done.12.list_a_ref
  132.5 1.3 collective-permute-start.5
  133.9 1.8 collective-permute-start.10
  135.6 0.0 copy-start
  135.6 0.0 copy-start.3
  135.7 0.0 copy-start.4
  135.7 1.6 collective-permute-start.11
  137.2 25.2 %guest_attention.5 = (bf16[1056,256]{1,0:T(8,128)(2,1)S(1)}, bf16[1056,256]{1,0:T(8,128)(2,1)S(1)}) custom-call(s32[256]{0:T(256)S(1)} %collective-permute-done.12.list_a_ref, s32[256]{0:T(256)S(1)} %collective-permute-done.13.list_b_ref, bf16[256,1024]{1,0:T(8,128)(2,1)S(1)} %collective-permute-done.14.q_a_ref, ...), custom_call_target="tpu_custom_call" | custom-call | flops 1610612736 | bytes 4194304 | tf_op jit(solution)/shard_map/guest_attention/pallas_call | solution.py:311
  162.4 1.3 collective-permute-start.16
  163.8 1.5 collective-permute-start.17
  165.9 12.8 %own_attention.1.refs_0_ = bf16[1056,256]{1,0:T(8,128)(2,1)S(1)} custom-call(s32[1]{0:T(128)S(6)} %copy.15.span_live_ref, s32[256]{0:T(256)S(1)} %bitcast.9, bf16[256,1024]{1,0:T(8,128)(2,1)S(1)} %copy-done.4, bf16[2,256,16,128]{3,2,1,0:T(8,128)(2,1)S(1)} %copy-done.3, bf16[2,256,128]{2,1,0:T(8,128)(2,1)S(1)} %copy-done), custom_call_target="tpu_custom_call" | custom-call | flops 1073741824 | bytes 4194304 | tf_op jit(solution)/shard_map/own_attention/pallas_call | solution.py:296
  178.7 0.0 collective-permute-done.5.refs_2_
  178.7 0.0 collective-permute-done.16.refs_5_
  178.8 9.5 %project.1 = bf16[256,4096]{1,0:T(8,128)(2,1)} custom-call(s32[1]{0:T(128)} %bitcast.me_ref, s32[1]{0:T(128)S(6)} %copy.15.span_live_ref, bf16[1056,256]{1,0:T(8,128)(2,1)S(1)} %own_attention.1.refs_0_, bf16[1056,256]{1,0:T(8,128)(2,1)S(1)} %collective-permute-done.4.refs_1_, bf16[1056,256]{1,0:T(8,128)(2,1)S(1)} %collective-permute-done.5.refs_2_, ...), custom_call_target="tpu_custom_call" | custom-call | flops 2147483648 | bytes 10485760 | tf_op jit(solution)/shard_map/project/pallas_call | solution.py:224
  188.2 0.0 reduce-scatter.2.cloned.1.call-update
  188.3 0.6 copy-done.1
  188.9 0.6 pack_blocks.1
  189.5 22.2 %all_to_all.5 = bf16[2,4,8,16,128]{4,3,2,0,1:T(8,128)(2,1)S(1)} all-to-all(bf16[2,4,8,16,128]{4,3,2,0,1:T(8,128)(2,1)S(1)} %copy.12), channel_id=1, replica_groups=mesh['pods'=2,'inst'=4,'tp'=4] {'inst'}, dimensions={1} | all-to-all | bytes 524288 | tf_op jit(solution)/shard_map/all_to_all | solution.py:338
  211.7 0.7 copy.13
  212.5 19.0 %reduce-scatter.2.cloned.1.call-done = bf16[64,4096]{1,0:T(8,128)(2,1)} async-done(((bf16[256,4096]{1,0:T(8,128)(2,1)}), bf16[64,4096]{1,0:T(8,128)(2,1)}) %reduce-scatter.2.cloned.1.call-update) | async-done | bytes 524304 | tf_op jit(solution)/shard_map/reduce_scatter | solution.py:325
  (12 shorter events, 0.0 us)
Async XLA Ops:
  7.2 224.3 %reduce-scatter.2.cloned.1.call-start = ((), (), s32[]{:S(2)}) async-start(), calls=%async_computation.2 | async-start | bytes 2621440 | tf_op jit(solution)/shard_map/reduce_scatter | solution.py:325
  7.2 15.0 %collective-permute-start.2 = (bf16[256,1024]{1,0:T(8,128)(2,1)}, bf16[256,1024]{1,0:T(8,128)(2,1)S(1)}, u32[]{:S(2)}, u32[]{:S(2)}) collective-permute-start(bf16[256,1024]{1,0:T(8,128)(2,1)} %q_ref.1), channel_id=1, source_target_pairs={{0,4},{4,8},{8,12},{1,5},{5,9},{9,13},{2,6},{6,10},{10,14},{3,7},{... | collective-permute-start | bytes 1572872 | tf_op jit(solution)/shard_map/ppermute | solution.py:287
  10.7 15.8 %collective-permute-start.3 = (bf16[256,1024]{1,0:T(8,128)(2,1)}, bf16[256,1024]{1,0:T(8,128)(2,1)S(1)}, u32[]{:S(2)}, u32[]{:S(2)}) collective-permute-start(bf16[256,1024]{1,0:T(8,128)(2,1)} %q_ref.1), channel_id=1, source_target_pairs={{4,0},{8,4},{12,8},{5,1},{9,5},{13,9},{6,2},{10,6},{14,10},{7,3},{... | collective-permute-start | bytes 1572872 | tf_op jit(solution)/shard_map/ppermute | solution.py:287
  22.2 21.4 %collective-permute-start.8 = (bf16[256,1024]{1,0:T(8,128)(2,1)S(1)}, bf16[256,1024]{1,0:T(8,128)(2,1)S(1)}, u32[]{:S(2)}, u32[]{:S(2)}) collective-permute-start(bf16[256,1024]{1,0:T(8,128)(2,1)S(1)} %collective-permute-done.2.q_a_ref), channel_id=1, source_target_pairs={{0,4},{4,8},{8,12},{1,5},{5,9},{9,13},{2,6},{6,10},{10,14},{3,7},{... | collective-permute-start | bytes 1572872 | tf_op jit(solution)/shard_map/ppermute | solution.py:287
  26.5 21.7 %collective-permute-start.9 = (bf16[256,1024]{1,0:T(8,128)(2,1)S(1)}, bf16[256,1024]{1,0:T(8,128)(2,1)S(1)}, u32[]{:S(2)}, u32[]{:S(2)}) collective-permute-start(bf16[256,1024]{1,0:T(8,128)(2,1)S(1)} %collective-permute-done.3.q_b_ref), channel_id=1, source_target_pairs={{4,0},{8,4},{12,8},{5,1},{9,5},{13,9},{6,2},{10,6},{14,10},{7,3},{... | collective-permute-start | bytes 1572872 | tf_op jit(solution)/shard_map/ppermute | solution.py:287
  33.2 16.3 %collective-permute-start = (s32[256]{0:T(256)S(1)}, s32[256]{0:T(256)S(1)}, u32[]{:S(2)}, u32[]{:S(2)}) collective-permute-start(s32[256]{0:T(256)S(1)} %bitcast.14), channel_id=1, source_target_pairs={{0,4},{4,8},{8,12},{1,5},{5,9},{9,13},{2,6},{6,10},{10,14},{3,7},{... | collective-permute-start | bytes 3080 | tf_op jit(solution)/shard_map/ppermute | solution.py:287
  42.3 7.2 %collective-permute-start.1 = (s32[256]{0:T(256)S(1)}, s32[256]{0:T(256)S(1)}, u32[]{:S(2)}, u32[]{:S(2)}) collective-permute-start(s32[256]{0:T(256)S(1)} %bitcast.16), channel_id=1, source_target_pairs={{4,0},{8,4},{12,8},{5,1},{9,5},{13,9},{6,2},{10,6},{14,10},{7,3},{... | collective-permute-start | bytes 3080 | tf_op jit(solution)/shard_map/ppermute | solution.py:287
  43.6 92.0 %collective-permute-start.14 = (bf16[256,1024]{1,0:T(8,128)(2,1)S(1)}, bf16[256,1024]{1,0:T(8,128)(2,1)S(1)}, u32[]{:S(2)}, u32[]{:S(2)}) collective-permute-start(bf16[256,1024]{1,0:T(8,128)(2,1)S(1)} %collective-permute-done.8.q_a_ref), channel_id=1, source_target_pairs={{0,4},{4,8},{8,12},{1,5},{5,9},{9,13},{2,6},{6,10},{10,14},{3,7},{... | collective-permute-start | bytes 1572872 | tf_op jit(solution)/shard_map/ppermute | solution.py:287
  48.2 89.0 %collective-permute-start.15 = (bf16[256,1024]{1,0:T(8,128)(2,1)S(1)}, bf16[256,1024]{1,0:T(8,128)(2,1)S(1)}, u32[]{:S(2)}, u32[]{:S(2)}) collective-permute-start(bf16[256,1024]{1,0:T(8,128)(2,1)S(1)} %collective-permute-done.9.q_b_ref), channel_id=1, source_target_pairs={{4,0},{8,4},{12,8},{5,1},{9,5},{13,9},{6,2},{10,6},{14,10},{7,3},{... | collective-permute-start | bytes 1572872 | tf_op jit(solution)/shard_map/ppermute | solution.py:287
  49.5 1.6 copy-start.2
  73.6 90.1 %collective-permute-start.4 = (bf16[1056,256]{1,0:T(8,128)(2,1)S(1)}, bf16[1056,256]{1,0:T(8,128)(2,1)S(1)}, u32[]{:S(2)}, u32[]{:S(2)}) collective-permute-start(bf16[1056,256]{1,0:T(8,128)(2,1)S(1)} %get-tuple-element.8), channel_id=1, source_target_pairs={{0,4},{4,8},{8,12},{1,5},{5,9},{9,13},{2,6},{6,10},{10,14},{3,7},{... | collective-permute-start | bytes 1622024 | tf_op jit(solution)/shard_map/ppermute | solution.py:287
  75.0 34.4 %collective-permute-start.6 = (s32[256]{0:T(256)S(1)}, s32[256]{0:T(256)S(1)}, u32[]{:S(2)}, u32[]{:S(2)}) collective-permute-start(s32[256]{0:T(256)S(1)} %bitcast.18), channel_id=1, source_target_pairs={{0,8},{4,12},{1,9},{5,13},{2,10},{6,14},{3,11},{7,15},{16,24},{20,... | collective-permute-start | bytes 3080 | tf_op jit(solution)/shard_map/ppermute | solution.py:287
  108.1 12.6 %collective-permute-start.7 = (s32[256]{0:T(256)S(1)}, s32[256]{0:T(256)S(1)}, u32[]{:S(2)}, u32[]{:S(2)}) collective-permute-start(s32[256]{0:T(256)S(1)} %bitcast.19), channel_id=1, source_target_pairs={{8,0},{12,4},{9,1},{13,5},{10,2},{14,6},{11,3},{15,7},{24,16},{28,... | collective-permute-start | bytes 3080 | tf_op jit(solution)/shard_map/ppermute | solution.py:287
  109.4 23.2 %collective-permute-start.12 = (s32[256]{0:T(256)S(1)}, s32[256]{0:T(256)S(1)}, u32[]{:S(2)}, u32[]{:S(2)}) collective-permute-start(s32[256]{0:T(256)S(1)} %bitcast.17), channel_id=1, source_target_pairs={{0,12},{1,13},{2,14},{3,15},{16,28},{17,29},{18,30},{19,31}} | collective-permute-start | bytes 3080 | tf_op jit(solution)/shard_map/ppermute | solution.py:287
  120.7 13.1 %collective-permute-start.13 = (s32[256]{0:T(256)S(1)}, s32[256]{0:T(256)S(1)}, u32[]{:S(2)}, u32[]{:S(2)}) collective-permute-start(s32[256]{0:T(256)S(1)} %bitcast.15), channel_id=1, source_target_pairs={{12,0},{13,1},{14,2},{15,3},{28,16},{29,17},{30,18},{31,19}} | collective-permute-start | bytes 3080 | tf_op jit(solution)/shard_map/ppermute | solution.py:287
  132.5 46.2 %collective-permute-start.5 = (bf16[1056,256]{1,0:T(8,128)(2,1)S(1)}, bf16[1056,256]{1,0:T(8,128)(2,1)S(1)}, u32[]{:S(2)}, u32[]{:S(2)}) collective-permute-start(bf16[1056,256]{1,0:T(8,128)(2,1)S(1)} %get-tuple-element.9), channel_id=1, source_target_pairs={{4,0},{8,4},{12,8},{5,1},{9,5},{13,9},{6,2},{10,6},{14,10},{7,3},{... | collective-permute-start | bytes 1622024 | tf_op jit(solution)/shard_map/ppermute | solution.py:287
  133.9 44.9 %collective-permute-start.10 = (bf16[1056,256]{1,0:T(8,128)(2,1)S(1)}, bf16[1056,256]{1,0:T(8,128)(2,1)S(1)}, u32[]{:S(2)}, u32[]{:S(2)}) collective-permute-start(bf16[1056,256]{1,0:T(8,128)(2,1)S(1)} %get-tuple-element.10), channel_id=1, source_target_pairs={{0,8},{4,12},{1,9},{5,13},{2,10},{6,14},{3,11},{7,15},{16,24},{20,... | collective-permute-start | bytes 1622024 | tf_op jit(solution)/shard_map/ppermute | solution.py:287
  135.6 30.3 %copy-start = (bf16[2,256,128]{2,1,0:T(8,128)(2,1)S(1)}, bf16[2,256,128]{2,1,0:T(8,128)(2,1)}, u32[]{:S(2)}) copy-start(bf16[2,256,128]{2,1,0:T(8,128)(2,1)} %span_ref.3) | copy-start | bytes 393220
  135.6 30.3 %copy-start.3 = (bf16[2,256,16,128]{3,2,1,0:T(8,128)(2,1)S(1)}, bf16[2,256,16,128]{3,2,1,0:T(8,128)(2,1)}, u32[]{:S(2)}) copy-start(bf16[2,256,16,128]{3,2,1,0:T(8,128)(2,1)} %store_ref.7) | copy-start | bytes 6291460
  135.7 30.3 %copy-start.4 = (bf16[256,1024]{1,0:T(8,128)(2,1)S(1)}, bf16[256,1024]{1,0:T(8,128)(2,1)}, u32[]{:S(2)}) copy-start(bf16[256,1024]{1,0:T(8,128)(2,1)} %q_ref.1) | copy-start | bytes 1572868
  135.7 43.1 %collective-permute-start.11 = (bf16[1056,256]{1,0:T(8,128)(2,1)S(1)}, bf16[1056,256]{1,0:T(8,128)(2,1)S(1)}, u32[]{:S(2)}, u32[]{:S(2)}) collective-permute-start(bf16[1056,256]{1,0:T(8,128)(2,1)S(1)} %get-tuple-element.11), channel_id=1, source_target_pairs={{8,0},{12,4},{9,1},{13,5},{10,2},{14,6},{11,3},{15,7},{24,16},{28,... | collective-permute-start | bytes 1622024 | tf_op jit(solution)/shard_map/ppermute | solution.py:287
  162.4 16.3 %collective-permute-start.16 = (bf16[1056,256]{1,0:T(8,128)(2,1)S(1)}, bf16[1056,256]{1,0:T(8,128)(2,1)S(1)}, u32[]{:S(2)}, u32[]{:S(2)}) collective-permute-start(bf16[1056,256]{1,0:T(8,128)(2,1)S(1)} %get-tuple-element.12), channel_id=1, source_target_pairs={{0,12},{1,13},{2,14},{3,15},{16,28},{17,29},{18,30},{19,31}} | collective-permute-start | bytes 1622024 | tf_op jit(solution)/shard_map/ppermute | solution.py:287
  163.8 15.0 %collective-permute-start.17 = (bf16[1056,256]{1,0:T(8,128)(2,1)S(1)}, bf16[1056,256]{1,0:T(8,128)(2,1)S(1)}, u32[]{:S(2)}, u32[]{:S(2)}) collective-permute-start(bf16[1056,256]{1,0:T(8,128)(2,1)S(1)} %get-tuple-element.13), channel_id=1, source_target_pairs={{12,0},{13,1},{14,2},{15,3},{28,16},{29,17},{30,18},{31,19}} | collective-permute-start | bytes 1622024 | tf_op jit(solution)/shard_map/ppermute | solution.py:287
  188.2 0.7 copy-start.1
Sparse Core Ops, SparseCore 0:
  188.4 43.0 reduce-scatter.1

commit v2 on v1

v2 whole, which is shorter than its diff:
```python
import functools
import math

import jax
import jax.numpy as jnp
from jax import lax
from jax.experimental import pallas as pl
from jax.experimental.pallas import tpu as pltpu
from jax.sharding import PartitionSpec as P

LOW = -1e30
TILE = 16
VMEM_LIMIT = 48 * 1024 * 1024

SMEM = pl.BlockSpec(memory_space=pltpu.SMEM)
VMEM = pl.BlockSpec(memory_space=pltpu.VMEM)


def round_up(number, step):
    return -(-number // step) * step


def route_kernel(live_ref, holders_ref, slots_ref, lists_ref):
    peers, width = lists_ref.shape
    number = holders_ref.shape[1]
    padded = round_up(peers, 16)
    holder = lax.broadcasted_iota(jnp.int32, (padded, number), 0)
    entry = lax.broadcasted_iota(jnp.int32, (padded, number), 1)
    hot = (holders_ref[...] == holder) & (entry < live_ref[0])
    ones = jnp.where(hot, 1.0, 0.0)
    earlier = lax.broadcasted_iota(jnp.int32, (number, number), 0) < lax.broadcasted_iota(
        jnp.int32, (number, number), 1
    )
    ranks = jnp.dot(
        ones.astype(jnp.bfloat16),
        jnp.where(earlier, 1.0, 0.0).astype(jnp.bfloat16),
        preferred_element_type=jnp.float32,
    )
    rank = jnp.sum(ranks * ones, axis=0, keepdims=True)
    rank = jnp.broadcast_to(rank, (8, number)).T[:, :1].astype(jnp.int32)
    place = lax.broadcasted_iota(jnp.int32, (number, width), 1) == rank
    slots = jnp.where(hot, slots_ref[...], 0).astype(jnp.float32)
    lists = jnp.dot(
        slots.astype(jnp.bfloat16),
        jnp.where(place, 1.0, 0.0).astype(jnp.bfloat16),
        preferred_element_type=jnp.float32,
    )
    counts = jnp.sum(ones, axis=1, keepdims=True)
    last = lax.broadcasted_iota(jnp.int32, (padded, width), 1) == width - 1
    lists_ref[...] = jnp.where(last, counts, lists)[:peers].astype(jnp.int32)


def route(live, holders, slots, peers, cap):
    width = round_up(cap + 1, 128)
    return pl.pallas_call(
        route_kernel,
        out_shape=jax.ShapeDtypeStruct((peers, width), jnp.int32),
        in_specs=[SMEM, VMEM, VMEM],
        out_specs=VMEM,
        name="route",
    )(live, holders, slots)


def score(keys, qt_ref, g):
    return jnp.dot(keys, qt_ref[g], preferred_element_type=jnp.float32)


def absorb_tile(keys, values, qt_ref, max_ref, acc_ref, scale, s, tail=None, middle=None, mask=None):
    heads = max_ref.shape[0]
    for g in range(heads):
        if g + 1 < heads:
            following = score(keys, qt_ref, g + 1)
        elif tail is not None:
            tail()
        if mask is not None:
            s = jnp.where(mask, s, LOW)
        old = max_ref[g]
        new = jnp.maximum(old, jnp.max(s, axis=0, keepdims=True))
        p = jnp.exp2((s - new) * scale).astype(jnp.bfloat16)
        update = jnp.dot(values, p, preferred_element_type=jnp.float32)
        acc_ref[g] = acc_ref[g] * jnp.exp2((old - new) * scale) + update
        max_ref[g] = new
        if middle is not None and g == heads // 2:
            middle()
        s = following


def transposed_values(values, valid_keys):
    keys = values.shape[0]
    row = lax.broadcasted_iota(jnp.int32, (16, keys), 0)
    col = lax.broadcasted_iota(jnp.int32, (16, keys), 1)
    marks = jnp.where((row == 0) & (col < valid_keys), 1.0, 0.0).astype(jnp.bfloat16)
    return jnp.concatenate([values.T, marks], axis=0)


def absorb_blocks(slot, count, store_ref, qt_ref, k_ref, v_ref, vt_ref, s_ref, max_ref, acc_ref, scale):
    block_rows = store_ref.shape[2]

    def fetch(tile, into):
        for j in range(TILE):
            index = tile * TILE + j
            here = slot(jnp.maximum(jnp.minimum(index, count - 1), 0))
            k_ref[into, j * block_rows : (j + 1) * block_rows, :] = store_ref[0, here]
            block = store_ref[1, here]
            v_ref[j * block_rows : (j + 1) * block_rows, :] = jnp.where(
                index < count, block, jnp.zeros_like(block)
            )
        vt_ref[into] = transposed_values(v_ref[...], (count - tile * TILE) * block_rows)

    @pl.when(count > 0)
    def _():
        fetch(0, 0)
        s_ref[...] = score(k_ref[0], qt_ref, 0)

        def step(tile, carry):
            now = lax.rem(tile, 2)
            later = 1 - now

            def tail():
                s_ref[...] = score(k_ref[later], qt_ref, 0)

            absorb_tile(
                k_ref[now], vt_ref[now], qt_ref, max_ref, acc_ref, scale, s_ref[...],
                tail=tail, middle=lambda: fetch(tile + 1, later),
            )
            return carry

        lax.fori_loop(0, (count + TILE - 1) // TILE, step, 0)


def begin(q_ref, qt_ref, max_ref, acc_ref):
    heads = max_ref.shape[0]
    head_dim = qt_ref.shape[1]
    max_ref[...] = jnp.full_like(max_ref, LOW)
    acc_ref[...] = jnp.zeros_like(acc_ref)
    for g in range(heads):
        qt_ref[g] = q_ref[:, g * head_dim : (g + 1) * head_dim].T


def finish(out_ref, max_ref, acc_ref, scale):
    heads = max_ref.shape[0]
    head_dim = acc_ref.shape[1] - 16
    logs = []
    for g in range(heads):
        total = acc_ref[g, head_dim : head_dim + 8, :][:1]
        some = total > 0.0
        inverse = jnp.where(some, 1.0 / jnp.where(some, total, 1.0), 0.0)
        out_ref[g * head_dim : (g + 1) * head_dim, :] = (
            acc_ref[g, :head_dim, :] * inverse
        ).astype(jnp.bfloat16)
        logs.append(
            jnp.where(some, max_ref[g] * scale + jnp.log2(jnp.where(some, total, 1.0)), LOW)
        )
    logs = jnp.concatenate(logs, axis=0)
    first = logs.astype(jnp.bfloat16).astype(jnp.float32)
    rest = logs - first
    second = rest.astype(jnp.bfloat16).astype(jnp.float32)
    third = rest - second
    pieces = jnp.concatenate([first, second, third, jnp.zeros_like(first)], axis=0)
    out_ref[heads * head_dim :, :] = pieces.astype(jnp.bfloat16)


def own_kernel(
    scale, me_ref, span_live_ref, list_ref, q_ref, store_ref, span_ref, out_ref,
    qt_ref, k_ref, v_ref, vt_ref, s_ref, max_ref, acc_ref,
):
    me = me_ref[0]
    begin(q_ref, qt_ref, max_ref, acc_ref)
    rows = q_ref.shape[0]
    keys = span_ref.shape[1]
    key = lax.broadcasted_iota(jnp.int32, (keys, rows), 0)
    row = lax.broadcasted_iota(jnp.int32, (keys, rows), 1)
    absorb_tile(
        span_ref[0], transposed_values(span_ref[1], keys), qt_ref, max_ref, acc_ref, scale,
        score(span_ref[0], qt_ref, 0), mask=(key <= row) & (key < span_live_ref[0]),
    )
    absorb_blocks(
        lambda index: list_ref[me, index], list_ref[me, list_ref.shape[1] - 1],
        store_ref, qt_ref, k_ref, v_ref, vt_ref, s_ref, max_ref, acc_ref, scale,
    )
    finish(out_ref.at[0], max_ref, acc_ref, scale)


def guest_kernel(
    scale, me_ref, lists_ref, q_ref, store_ref, kept_ref, out_ref,
    qt_ref, k_ref, v_ref, vt_ref, s_ref, max_ref, acc_ref,
):
    me = me_ref[0]
    peers = lists_ref.shape[0]
    guest = lax.rem(me + 1 + pl.program_id(0), peers)
    begin(q_ref.at[0], qt_ref, max_ref, acc_ref)
    absorb_blocks(
        lambda index: lists_ref[guest, me, index], lists_ref[guest, me, lists_ref.shape[2] - 1],
        store_ref, qt_ref, k_ref, v_ref, vt_ref, s_ref, max_ref, acc_ref, scale,
    )
    finish(out_ref.at[0], max_ref, acc_ref, scale)


def attention_scratch(heads, rows, head_dim, block_rows):
    keys = TILE * block_rows
    return [
        pltpu.VMEM((heads, head_dim, rows), jnp.bfloat16),
        pltpu.VMEM((2, keys, head_dim), jnp.bfloat16),
        pltpu.VMEM((keys, head_dim), jnp.bfloat16),
        pltpu.VMEM((2, head_dim + 16, keys), jnp.bfloat16),
        pltpu.VMEM((keys, rows), jnp.float32),
        pltpu.VMEM((heads, 1, rows), jnp.float32),
        pltpu.VMEM((heads, head_dim + 16, rows), jnp.float32),
    ]


def attention_cost(rows, keys, head_dim, heads):
    return pl.CostEstimate(
        flops=4 * rows * keys * head_dim * heads,
        bytes_accessed=4 * 1024 * 1024,
        transcendentals=rows * keys * heads,
    )


def project_kernel(span_live_ref, parts_ref, weight_ref, out_ref, att_ref):
    rows, features = att_ref.shape
    peers = parts_ref.shape[0]

    @pl.when(pl.program_id(0) == 0)
    def _():
        heads = (parts_ref.shape[1] - features) // 4
        head_dim = features // heads
        logs = []
        for h in range(peers):
            pieces = parts_ref[h, features:, :].astype(jnp.float32)
            logs.append(pieces[:heads] + pieces[heads : 2 * heads] + pieces[2 * heads : 3 * heads])
        top = functools.reduce(jnp.maximum, logs)
        weights = [jnp.exp2(log - top) for log in logs]
        inverse = 1.0 / functools.reduce(jnp.add, weights)
        row = lax.broadcasted_iota(jnp.int32, (heads, rows), 1)
        inverse = jnp.where(row < span_live_ref[0], inverse, 0.0)
        weights = [weight * inverse for weight in weights]
        for g in range(heads):
            total = jnp.zeros((head_dim, rows), jnp.float32)
            for h in range(peers):
                part = parts_ref[h, g * head_dim : (g + 1) * head_dim, :]
                total += part.astype(jnp.float32) * weights[h][g : g + 1]
            att_ref[:, g * head_dim : (g + 1) * head_dim] = total.T.astype(jnp.bfloat16)

    out_ref[...] = jnp.dot(
        att_ref[...], weight_ref[...], preferred_element_type=jnp.float32
    ).astype(jnp.bfloat16)


def project(span_live, parts, out_weight):
    features, outputs = out_weight.shape
    rows = parts.shape[2]
    width = 512
    return pl.pallas_call(
        project_kernel,
        out_shape=jax.ShapeDtypeStruct((rows, outputs), jnp.bfloat16),
        grid_spec=pltpu.PrefetchScalarGridSpec(
            num_scalar_prefetch=1,
            grid=(outputs // width,),
            in_specs=[
                pl.BlockSpec(parts.shape, lambda i, *_: (0, 0, 0)),
                pl.BlockSpec((features, width), lambda i, *_: (0, i)),
            ],
            out_specs=pl.BlockSpec((rows, width), lambda i, *_: (0, i)),
            scratch_shapes=[pltpu.VMEM((rows, features), jnp.bfloat16)],
        ),
        compiler_params=pltpu.CompilerParams(vmem_limit_bytes=VMEM_LIMIT),
        cost_estimate=pl.CostEstimate(
            flops=2 * rows * features * outputs,
            bytes_accessed=2 * (features + rows) * outputs,
            transcendentals=0,
        ),
        name="project",
    )(span_live, parts, out_weight)


def pack_kernel(span_live_ref, owners_ref, span_ref, out_ref, counts_ref):
    peers = out_ref.shape[1]
    block_rows, head_dim = out_ref.shape[3:]
    out_ref[...] = jnp.zeros_like(out_ref)
    for k in range(peers):
        counts_ref[k] = 0
    row = lax.broadcasted_iota(jnp.int32, (block_rows, head_dim), 0)
    for b in range(span_ref.shape[1] // block_rows):
        owner = owners_ref[b]
        rank = counts_ref[owner]
        counts_ref[owner] = rank + 1
        keep = row + b * block_rows < span_live_ref[0]
        for side in range(2):
            block = span_ref[side, b * block_rows : (b + 1) * block_rows, :]
            out_ref[side, owner, rank] = jnp.where(keep, block, jnp.zeros_like(block))


def shards(
    queries,
    cache_store,
    span_cache,
    out_weight,
    prefix_blocks,
    span_lengths,
    hit_holders,
    hit_slots,
    store_owners,
):
    peers = lax.axis_size("inst")
    block_rows, head_dim = cache_store.shape[2:]
    rows, columns = queries.shape
    heads = columns // head_dim
    block_max = hit_slots.shape[1]
    cap = max(2, block_max * 5 // (4 * peers))
    new_count = rows // block_rows
    push_cap = max(2, 2 * new_count // peers)
    scale = math.log2(math.e) / math.sqrt(head_dim)
    me = lax.axis_index("inst").reshape(1)
    part_rows = heads * head_dim + 4 * heads
    parts_shape = jax.ShapeDtypeStruct((peers, part_rows, rows), jnp.bfloat16)

    all_queries = lax.all_gather(queries, "inst")
    lists = route(prefix_blocks, hit_holders.reshape(1, -1), hit_slots, peers, cap)
    all_lists = lax.all_gather(lists, "inst")

    whole_store = pl.BlockSpec(cache_store.shape, lambda i, *_: (0, 0, 0, 0))
    own = pl.pallas_call(
        functools.partial(own_kernel, scale),
        out_shape=parts_shape,
        grid_spec=pltpu.PrefetchScalarGridSpec(
            num_scalar_prefetch=3,
            grid=(1,),
            in_specs=[
                pl.BlockSpec((rows, columns), lambda i, *_: (0, 0)),
                whole_store,
                pl.BlockSpec(span_cache.shape, lambda i, *_: (0, 0, 0)),
            ],
            out_specs=pl.BlockSpec((1, part_rows, rows), lambda i, at, *_: (at[0], 0, 0)),
            scratch_shapes=attention_scratch(heads, rows, head_dim, block_rows),
        ),
        compiler_params=pltpu.CompilerParams(vmem_limit_bytes=VMEM_LIMIT),
        cost_estimate=attention_cost(rows, 8 * rows, head_dim, heads),
        name="own_attention",
    )(me, span_lengths, lists, queries, cache_store, span_cache)

    parts = pl.pallas_call(
        functools.partial(guest_kernel, scale),
        out_shape=parts_shape,
        grid_spec=pltpu.PrefetchScalarGridSpec(
            num_scalar_prefetch=2,
            grid=(peers - 1,),
            in_specs=[
                pl.BlockSpec(
                    (1, rows, columns), lambda i, at, *_: (lax.rem(at[0] + 1 + i, peers), 0, 0)
                ),
                whole_store,
                pl.BlockSpec(memory_space=pl.ANY),
            ],
            out_specs=pl.BlockSpec(
                (1, part_rows, rows), lambda i, at, *_: (lax.rem(at[0] + 1 + i, peers), 0, 0)
            ),
            scratch_shapes=attention_scratch(heads, rows, head_dim, block_rows),
        ),
        input_output_aliases={4: 0},
        compiler_params=pltpu.CompilerParams(vmem_limit_bytes=VMEM_LIMIT),
        cost_estimate=attention_cost(rows, 16 * rows, head_dim, heads),
        name="guest_attention",
    )(me, all_lists, all_queries, cache_store, own)

    parts = lax.all_to_all(parts, "inst", split_axis=0, concat_axis=0, tiled=True)
    partial = project(span_lengths, parts, out_weight)
    projected = lax.psum_scatter(partial, "tp", scatter_dimension=0, tiled=True)

    outgoing = pl.pallas_call(
        pack_kernel,
        out_shape=jax.ShapeDtypeStruct(
            (2, peers, push_cap, block_rows, head_dim), jnp.bfloat16
        ),
        in_specs=[SMEM, SMEM, VMEM],
        out_specs=VMEM,
        scratch_shapes=[pltpu.SMEM((peers,), jnp.int32)],
        compiler_params=pltpu.CompilerParams(vmem_limit_bytes=VMEM_LIMIT),
        name="pack_blocks",
    )(span_lengths, store_owners.reshape(-1), span_cache)
    incoming = lax.all_to_all(outgoing, "inst", split_axis=1, concat_axis=1, tiled=True)
    pushed_blocks = incoming.reshape(2, peers * push_cap, block_rows, head_dim)
    return (projected, pushed_blocks)


def solution(mesh):
    return jax.shard_map(
        shards,
        mesh=mesh,
        in_specs=(
            P(("pods", "inst"), "tp"),
            P(None, ("pods", "inst"), None, "tp"),
            P(None, ("pods", "inst"), "tp"),
            P("tp", None),
            P(("pods", "inst")),
            P(("pods", "inst")),
            P(("pods", "inst"), None, None),
            P(("pods", "inst"), None),
            P(("pods", "inst"), None, None),
        ),
        out_specs=(P(("pods", "inst", "tp"), None), P(None, ("pods", "inst"), None, "tp")),
        check_vma=False,
    )
```

time: 238 us -> 190 us (0.80); the launches traced: 238 us -> 186 us
  starting transfers between devices: 82.4 us -> 0.08 us
  blocking collectives: 22.2 us -> 78.2 us
  Pallas kernels: 85 us -> 42.7 us
  waiting for transfers between devices: 29.2 us -> 41.1 us
  local copies, waits for them, and re-layouts: 3.82 us -> 8.78 us
    ppermute x18 -> x0, starting transfers between devices: 82.3 us -> none  [shift(): return lax.ppermute(value, 'inst', pairs)]
    all_to_all x0 -> x1, blocking collectives: none -> 53.5 us  [shards(): lax.all_to_all(parts, 'inst', split_axis=0, concat_axis=0, tiled=True)]
    pallas_call x6 -> x4, Pallas kernels: 84.4 us -> 42.1 us  [the longest x1 26.3 us: shards(): pl.pallas_call(functools.partial(guest_kernel, scale), out_shape=parts_sh...]
    all_gather x0 -> x1, waiting for transfers between devices: none -> 21.8 us  [shards(): all_queries = lax.all_gather(queries, 'inst')]
    all_gather x0 -> x1, blocking collectives: none -> 13.5 us  [shards(): all_lists = lax.all_gather(lists, 'inst')]
    all_to_all x1, blocking collectives: 22.2 us -> 11.3 us  [shards(): lax.all_to_all(outgoing, 'inst', split_axis=1, concat_axis=1, tiled=True)]
    ppermute x18 -> x0, waiting for transfers between devices: 10.2 us -> none  [shift(): return lax.ppermute(value, 'inst', pairs)]
    unnamed x10 -> x18, local copies, waits for them, and re-layouts: 2.24 us -> 8.04 us
  transfers between devices with their start and end apart: 19 -> 2, of which waited for: 2 -> 2; matrix products, arithmetic and copies ran while one was open for 1% -> 0% of each run, Pallas kernels for 32% -> 4%
where the time goes in v2:
time: 190 us; the launch traced here: 186 us
  blocking collectives  78.2 us (41%)
  Pallas kernels  42.7 us (22%)
  waiting for transfers between devices  41.1 us (22%)
  between operations  15.4 us (8%)
  local copies, waits for them, and re-layouts  8.78 us (5%)
    all_to_all x1, blocking collectives, shards(): lax.all_to_all(parts, 'inst', split_axis=0, concat_axis=0, tiled=True)  53.5 us
    pallas_call x1, Pallas kernels, shards(): pl.pallas_call(functools.partial(guest_kernel, scale), out_shape=parts_sh...  26.3 us
    all_gather x1, waiting for transfers between devices, shards(): all_queries = lax.all_gather(queries, 'inst')  21.8 us
    reduce_scatter x1, waiting for transfers between devices, shards(): projected = lax.psum_scatter(partial, 'tp', scatter_dimension=0, tiled=True)  18.6 us
    all_gather x1, blocking collectives, shards(): all_lists = lax.all_gather(lists, 'inst')  13.5 us
    all_to_all x1, blocking collectives, shards(): lax.all_to_all(outgoing, 'inst', split_axis=1, concat_axis=1, tiled=True)  11.3 us
    pallas_call x1, Pallas kernels, project(): pl.pallas_call(project_kernel, out_shape=jax.ShapeDtypeStruct((rows, outp...  9.15 us
    unnamed x18, local copies, waits for them, and re-layouts  8.04 us
  transfers between devices with their start and end apart: 2, of which 2 were waited for; matrix products, arithmetic and copies ran while one was open for 0% of the time, Pallas kernels for 4%

profile of v2, /device:TPU:4, one launch (start us, length us, event | category | flops | bytes accessed | tf_op | source)
XLA Modules:
  0.0 186.3 jit_solution(18245641896735876368)
XLA Ops:
  7.2 0.0 all-gather.5.cloned.1.call-start
  7.2 0.7 all-gather.5.cloned.1.call-update
  7.9 0.0 reduce-scatter.2.cloned.1.call-start
  9.2 2.0 %route.1.list_ref = s32[4,256]{1,0:T(4,128)} custom-call(s32[1]{0:T(128)S(6)} %copy.16.live_ref, s32[1,512]{1,0:T(1,128)} %bitcast.10, s32[1,512]{1,0:T(1,128)} %slots_ref.1), custom_call_target="tpu_custom_call" | custom-call | tf_op jit(solution)/shard_map/route/pallas_call | solution.py:55
  11.2 13.5 %all-gather.2.lists_ref = s32[4,4,256]{2,1,0:T(4,128)S(1)} all-gather(s32[1,4,256]{2,1,0:T(4,128)} %bitcast.6), channel_id=2, replica_groups=mesh['pods'=2,'inst'=4,'tp'=4] {'inst'}, dimensions={0}, use_global_device_ids=true | all-gather | bytes 20480 | tf_op jit(solution)/shard_map/all_gather | solution.py:320
  24.7 0.0 copy-start.1
  24.7 1.0 copy-done.1
  25.8 0.0 copy-start.2
  25.8 0.9 copy-done.2
  26.7 0.0 copy-start.4
  26.7 0.7 copy-done.4
  27.3 0.0 copy-start.6
  27.3 1.6 copy-done.6
  28.9 0.0 copy-start.7
  28.9 4.7 %own_attention.1.kept_ref = bf16[4,1056,256]{2,1,0:T(8,128)(2,1)S(1)} custom-call(s32[1]{0:T(128)} %bitcast.me_ref, s32[1]{0:T(128)S(6)} %copy.17.span_live_ref, s32[4,256]{1,0:T(4,128)S(1)} %copy-done.4, bf16[256,1024]{1,0:T(8,128)(2,1)S(1)} %copy-done.1, bf16[2,256,16,128]{3,2,1,0:T(8,128)(2,1)S(1)} %copy-done.6, bf16[2,256,128]{2,1,0:T(8,128)(2,1)S(1)} %copy-done.2), custom_call_target="tpu_custom_call" | custom-call | flops 2147483648 | bytes 4194304 | tf_op jit(solution)/shard_map/own_attention/pallas_call | solution.py:323
  33.6 0.0 copy-start
  33.6 1.3 copy-done
  35.0 21.8 %all-gather.5.cloned.1.call-done = bf16[1024,1024]{1,0:T(8,128)(2,1)} async-done(((bf16[256,1024]{1,0:T(8,128)(2,1)}), bf16[1024,1024]{1,0:T(8,128)(2,1)}) %all-gather.5.cloned.1.call-update) | async-done | bytes 2097168 | tf_op jit(solution)/shard_map/all_gather | solution.py:318
  56.8 0.0 copy-done.7
  56.8 0.0 copy-start.8
  56.8 1.6 copy-done.8
  58.4 26.3 %guest_attention.1 = bf16[4,1056,256]{2,1,0:T(8,128)(2,1)} custom-call(s32[1]{0:T(128)} %bitcast.me_ref, s32[4,4,256]{2,1,0:T(4,128)S(1)} %all-gather.2.lists_ref, bf16[4,256,1024]{2,1,0:T(8,128)(2,1)S(1)} %bitcast.8, bf16[2,256,16,128]{3,2,1,0:T(8,128)(2,1)S(1)} %copy-done.7, bf16[4,1056,256]{2,1,0:T(8,128)(2,1)} %copy-done), custom_call_target="tpu_custom_call", output_to_operand_aliasing={{}: (4, {})} | custom-call | flops 4294967296 | bytes 4194304 | tf_op jit(solution)/shard_map/guest_attention/pallas_call | solution.py:342
  84.7 53.5 %all_to_all.10.parts_ref = bf16[4,1056,256]{2,1,0:T(8,128)(2,1)S(1)} all-to-all(bf16[4,1056,256]{2,1,0:T(8,128)(2,1)} %guest_attention.1), channel_id=1, replica_groups=mesh['pods'=2,'inst'=4,'tp'=4] {'inst'}, dimensions={0} | all-to-all | bytes 4325376 | tf_op jit(solution)/shard_map/all_to_all | solution.py:366
  138.2 0.0 copy-start.5
  138.2 9.1 %project.1 = bf16[256,4096]{1,0:T(8,128)(2,1)} custom-call(s32[1]{0:T(128)S(6)} %copy.17.span_live_ref, bf16[4,1056,256]{2,1,0:T(8,128)(2,1)S(1)} %all_to_all.10.parts_ref, bf16[1024,4096]{1,0:T(8,128)(2,1)} %weight_ref.1), custom_call_target="tpu_custom_call" | custom-call | flops 2147483648 | bytes 10485760 | tf_op jit(solution)/shard_map/project/pallas_call | solution.py:254
  147.3 0.0 copy-start.3
  147.3 0.0 reduce-scatter.2.cloned.1.call-update
  147.4 0.0 copy-done.5
  147.4 0.9 copy-done.3
  148.2 0.6 pack_blocks.1
  148.9 11.3 %all_to_all.11 = bf16[2,4,8,16,128]{4,3,2,0,1:T(8,128)(2,1)S(1)} all-to-all(bf16[2,4,8,16,128]{4,3,2,0,1:T(8,128)(2,1)S(1)} %copy.13), channel_id=1, replica_groups=mesh['pods'=2,'inst'=4,'tp'=4] {'inst'}, dimensions={1} | all-to-all | bytes 524288 | tf_op jit(solution)/shard_map/all_to_all | solution.py:381
  160.2 0.7 copy.14
  160.9 18.6 %reduce-scatter.2.cloned.1.call-done = bf16[64,4096]{1,0:T(8,128)(2,1)} async-done(((bf16[256,4096]{1,0:T(8,128)(2,1)}), bf16[64,4096]{1,0:T(8,128)(2,1)}) %reduce-scatter.2.cloned.1.call-update) | async-done | bytes 524304 | tf_op jit(solution)/shard_map/reduce_scatter | solution.py:368
  (1 shorter events, 0.0 us)
Async XLA Ops:
  7.2 49.6 %all-gather.5.cloned.1.call-start = ((), (), s32[]{:S(2)}) async-start(), calls=%async_computation.4 | async-start | bytes 2621440 | tf_op jit(solution)/shard_map/all_gather | solution.py:318
  7.9 171.5 %reduce-scatter.2.cloned.1.call-start = ((), (), s32[]{:S(2)}) async-start(), calls=%async_computation.3 | async-start | bytes 2621440 | tf_op jit(solution)/shard_map/reduce_scatter | solution.py:368
  24.7 1.0 copy-start.1
  25.8 0.9 copy-start.2
  26.7 0.7 copy-start.4
  27.3 1.6 copy-start.6
  28.9 27.9 %copy-start.7 = (bf16[2,256,16,128]{3,2,1,0:T(8,128)(2,1)S(1)}, bf16[2,256,16,128]{3,2,1,0:T(8,128)(2,1)}, u32[]{:S(2)}) copy-start(bf16[2,256,16,128]{3,2,1,0:T(8,128)(2,1)} %store_ref.3) | copy-start | bytes 6291460
  33.6 1.4 copy-start
  56.8 1.6 copy-start.8
  138.2 9.2 %copy-start.5 = (s32[1,16,1]{1,2,0:T(1,128)S(1)}, s32[1,16,1]{1,2,0:T(1,128)}, u32[]{:S(2)}) copy-start(s32[1,16,1]{1,2,0:T(1,128)} %param.17) | copy-start | bytes 196
  147.3 0.9 copy-start.3
Sparse Core Ops, SparseCore 0:
  9.6 47.1 all-gather.4
  147.5 31.9 reduce-scatter.1
